TPU v7x, 32 devices: a whole 2x2x4 slice. The times are simulated.
32 devices in a mesh: col: 8 (over z, x), row: 4 (over y, core).
Axes of the slice: x: 2, y: 2, z: 4, core: 2. Of those that a mesh axis runs over, the one named last changes fastest.
Arguments:
- right_side: float32 [8, 256, 256], P('col'), may hold values from -6 to 6
- coupling: bfloat16 [2, 4, 256, 81920], P(None, 'row', None, 'col'), may hold values from -0.01953125 to 0.01953125
- child_solution: bfloat16 [81920, 256], P(('col', 'row')), may hold values from -6 to 6
- factor_blocks: bfloat16 [2, 4, 256, 8, 256], P(None, 'row', None, 'col'), may hold values from -1 to 1
- pattern: int32 [8, 8], replicated, may hold values from 0 to 1, as said below
- diag_inverse: bfloat16 [8, 256, 256], P('col'), may hold values from -0.375 to 0.375
Outputs:
- solved: bfloat16 [8, 256, 256], P('col')
Inputs may be any that keep to these rules, and one draw needn't show every extreme that they name: pattern[j, j - 1] = 1 for every j from 1 to 7; entries with k >= j are not read.
All inputs are finite; a program needn't handle non-finite values.
Results may differ from a plain program's by a relative error of at most 0.017.
Values may be sent and summed in bfloat16 or wider, within the bound.
A program may use at most 64 MiB of HBM per device.

v0:
```python
import jax
import jax.numpy as jnp
from jax import lax
from jax.sharding import PartitionSpec as P


def per_device(right_side, coupling, child_solution, factor_blocks, pattern, diag_inverse):
    nrow = lax.axis_size("row")
    ncol = lax.axis_size("col")
    row_index = lax.axis_index("row")
    col_index = lax.axis_index("col")
    brows = coupling.shape[0]
    blk_size = coupling.shape[2]
    kcols = coupling.shape[3]
    rhs_count = child_solution.shape[1]
    nblk = pattern.shape[0]
    group = ncol // nblk
    part_rows = blk_size // group
    my_block = col_index // group
    my_offset = col_index % group * part_rows
    flat = coupling.reshape(brows * blk_size, kcols)
    update = jnp.dot(
        flat,
        lax.all_gather(child_solution, "row", axis=0, tiled=True),
        preferred_element_type=jnp.float32,
    )
    update = update.reshape(brows, blk_size, rhs_count)
    rhs_part = right_side.reshape(part_rows, rhs_count)
    placed = lax.dynamic_update_slice(
        jnp.zeros((blk_size, rhs_count), jnp.float32), rhs_part, (my_offset, jnp.int32(0))
    )
    blocks = factor_blocks.reshape(brows, blk_size, part_rows)
    inv_rows = diag_inverse.reshape(part_rows, blk_size)

    def advance(j, solved):
        j_row = j % nrow
        j_arow = j // nrow
        flags = lax.dynamic_index_in_dim(pattern, j, 0, keepdims=False)
        flag = lax.dynamic_index_in_dim(flags, my_block, 0, keepdims=False)
        keep = (flag > 0) & (my_block < j)
        masked = jnp.where(keep, solved, jnp.zeros_like(solved))
        row_blocks = lax.dynamic_index_in_dim(blocks, j_arow, 0, keepdims=False)
        partial_value = jnp.dot(row_blocks, masked, preferred_element_type=jnp.float32)
        partial_value = partial_value + lax.dynamic_index_in_dim(update, j_arow, 0, keepdims=False)
        partial_value = jnp.where(my_block == j, placed, jnp.zeros_like(placed)) - partial_value
        partial_value = jnp.where(row_index == j_row, partial_value, jnp.zeros_like(partial_value))
        total = lax.psum(partial_value, ("col", "row"))
        fresh = jnp.dot(
            inv_rows, total.astype(jnp.bfloat16), preferred_element_type=jnp.float32
        ).astype(jnp.bfloat16)
        return jnp.where(my_block == j, fresh, solved)

    start_state = jnp.zeros((part_rows, rhs_count), jnp.bfloat16)
    solved = lax.fori_loop(0, nblk, advance, start_state)
    return solved.reshape(1, part_rows, rhs_count)


def solution(mesh):
    in_specs = (
        P("col", None, None),
        P(None, "row", None, "col"),
        P(("col", "row"), None),
        P(None, "row", None, "col", None),
        P(),
        P("col", None, None),
    )
    out_specs = P("col", None, None)
    return jax.shard_map(
        per_device, mesh=mesh, in_specs=in_specs, out_specs=out_specs, check_vma=False
    )
```

profile of v0, /device:TPU:0, one launch (start us, length us, event | category | flops | bytes accessed | tf_op | source)
XLA Modules:
  0.0 424.0 jit_solution(1928758109962869587)
XLA Ops:
  6.5 0.0 all-gather.2.cloned.1.call-start
  6.5 0.7 all-gather.2.cloned.1.call-update
  7.3 1.1 copy.7
  8.4 0.0 copy-start
  8.4 0.0 copy-start.1
  8.4 43.7 %all-gather.2.cloned.1.call-done = bf16[10240,256]{1,0:T(8,128)(2,1)} async-done(((bf16[2560,256]{1,0:T(8,128)(2,1)}), bf16[10240,256]{1,0:T(8,128)(2,1)}) %all-gather.2.cloned.1.call-update) | async-done | bytes 5242896 | tf_op jit(solution)/shard_map/all_gather | solution.py:24
  52.1 8.4 %fusion.12 = f32[2,256,256]{1,2,0:T(8,128)S(1)} fusion(bf16[2,1,256,10240]{3,2,1,0:T(8,128)(2,1)} %param.9, bf16[10240,256]{1,0:T(8,128)(2,1)} %all-gather.2.cloned.1.call-done), kind=kOutput, calls=%fused_computation.15 | convolution fusion | flops 2684354560 | bytes 16252928 | tf_op jit(solution)/shard_map/dot_general | solution.py:22
  60.5 0.0 copy-done
  60.5 0.0 copy-done.1
  60.5 355.9 %while.17 = (s32[]{:T(128)}, bf16[256,256]{0,1:T(8,128)(2,1)S(1)}, s32[]{:T(128)}, s32[]{:T(128)}, f32[256,256]{0,1:T(8,128)S(1)}, /*index=5*/bf16[2,256,256]{2,...) while((s32[]{:T(128)}, bf16[256,256]{0,1:T(8,128)(2,1)S(1)}, ...), condition=%wide.region_2.3_spmd.clone, body=%wide.region_0.2_spmd.clone.sunk | while | flops 67764248 | bytes 1969544 | solution.py:54
  60.5 1.3 dynamic_slice.47
  62.5 0.2 fusion.27
  62.7 42.9 %all-reduce.1 = bf16[256,256]{0,1:T(8,128)(2,1)S(1)} all-reduce(f32[256,256]{0,1:T(8,128)S(1)} %fusion.27), channel_id=1, replica_groups=mesh['col'=8,'row'=4] {'col','row'}, use_global_device_ids=true, to_apply=%region_1.1 | all-reduce | flops 65536 | bytes 393216 | tf_op jit(solution)/shard_map/while/body/eval_jaxpr/psum | solution.py:47
  105.6 0.2 fusion.28
  105.9 1.3 dynamic_slice.47
  107.8 0.2 fusion.27
  108.0 41.9 %all-reduce.1 = bf16[256,256]{0,1:T(8,128)(2,1)S(1)} all-reduce(f32[256,256]{0,1:T(8,128)S(1)} %fusion.27), channel_id=1, replica_groups=mesh['col'=8,'row'=4] {'col','row'}, use_global_device_ids=true, to_apply=%region_1.1 | all-reduce | flops 65536 | bytes 393216 | tf_op jit(solution)/shard_map/while/body/eval_jaxpr/psum | solution.py:47
  150.0 0.2 fusion.28
  150.2 1.3 dynamic_slice.47
  152.2 0.2 fusion.27
  152.4 41.8 %all-reduce.1 = bf16[256,256]{0,1:T(8,128)(2,1)S(1)} all-reduce(f32[256,256]{0,1:T(8,128)S(1)} %fusion.27), channel_id=1, replica_groups=mesh['col'=8,'row'=4] {'col','row'}, use_global_device_ids=true, to_apply=%region_1.1 | all-reduce | flops 65536 | bytes 393216 | tf_op jit(solution)/shard_map/while/body/eval_jaxpr/psum | solution.py:47
  194.2 0.2 fusion.28
  194.5 1.3 dynamic_slice.47
  196.5 0.2 fusion.27
  196.7 41.9 %all-reduce.1 = bf16[256,256]{0,1:T(8,128)(2,1)S(1)} all-reduce(f32[256,256]{0,1:T(8,128)S(1)} %fusion.27), channel_id=1, replica_groups=mesh['col'=8,'row'=4] {'col','row'}, use_global_device_ids=true, to_apply=%region_1.1 | all-reduce | flops 65536 | bytes 393216 | tf_op jit(solution)/shard_map/while/body/eval_jaxpr/psum | solution.py:47
  238.6 0.2 fusion.28
  238.9 1.3 dynamic_slice.47
  240.9 0.2 fusion.27
  241.1 41.8 %all-reduce.1 = bf16[256,256]{0,1:T(8,128)(2,1)S(1)} all-reduce(f32[256,256]{0,1:T(8,128)S(1)} %fusion.27), channel_id=1, replica_groups=mesh['col'=8,'row'=4] {'col','row'}, use_global_device_ids=true, to_apply=%region_1.1 | all-reduce | flops 65536 | bytes 393216 | tf_op jit(solution)/shard_map/while/body/eval_jaxpr/psum | solution.py:47
  282.9 0.2 fusion.28
  283.1 1.3 dynamic_slice.47
  285.1 0.2 fusion.27
  285.3 42.0 %all-reduce.1 = bf16[256,256]{0,1:T(8,128)(2,1)S(1)} all-reduce(f32[256,256]{0,1:T(8,128)S(1)} %fusion.27), channel_id=1, replica_groups=mesh['col'=8,'row'=4] {'col','row'}, use_global_device_ids=true, to_apply=%region_1.1 | all-reduce | flops 65536 | bytes 393216 | tf_op jit(solution)/shard_map/while/body/eval_jaxpr/psum | solution.py:47
  327.3 0.2 fusion.28
  327.6 1.3 dynamic_slice.47
  329.5 0.2 fusion.27
  329.8 41.7 %all-reduce.1 = bf16[256,256]{0,1:T(8,128)(2,1)S(1)} all-reduce(f32[256,256]{0,1:T(8,128)S(1)} %fusion.27), channel_id=1, replica_groups=mesh['col'=8,'row'=4] {'col','row'}, use_global_device_ids=true, to_apply=%region_1.1 | all-reduce | flops 65536 | bytes 393216 | tf_op jit(solution)/shard_map/while/body/eval_jaxpr/psum | solution.py:47
  371.5 0.2 fusion.28
  371.7 1.3 dynamic_slice.47
  373.7 0.2 fusion.27
  373.9 42.2 %all-reduce.1 = bf16[256,256]{0,1:T(8,128)(2,1)S(1)} all-reduce(f32[256,256]{0,1:T(8,128)S(1)} %fusion.27), channel_id=1, replica_groups=mesh['col'=8,'row'=4] {'col','row'}, use_global_device_ids=true, to_apply=%region_1.1 | all-reduce | flops 65536 | bytes 393216 | tf_op jit(solution)/shard_map/while/body/eval_jaxpr/psum | solution.py:47
  416.1 0.2 fusion.28
  416.4 0.8 copy.9
  (1 shorter events, 0.0 us)
Async XLA Ops:
  6.5 45.5 %all-gather.2.cloned.1.call-start = ((), (), s32[]{:S(2)}) async-start(), calls=%async_computation | async-start | bytes 6553600 | tf_op jit(solution)/shard_map/all_gather | solution.py:24
  8.4 52.1 %copy-start = (bf16[2,1,256,1,256]{4,2,3,1,0:T(8,128)(2,1)S(1)}, bf16[2,1,256,1,256]{4,2,3,1,0:T(8,128)(2,1)}, u32[]{:S(2)}) copy-start(bf16[2,1,256,1,256]{4,2,3,1,0:T(8,128)(2,1)} %param.11) | copy-start | bytes 786436
  8.4 52.1 %copy-start.1 = (bf16[1,256,256]{2,1,0:T(8,128)(2,1)S(1)}, bf16[1,256,256]{2,1,0:T(8,128)(2,1)}, u32[]{:S(2)}) copy-start(bf16[1,256,256]{2,1,0:T(8,128)(2,1)} %param.13) | copy-start | bytes 393220
Sparse Core Ops, SparseCore 0:
  8.9 43.1 all-gather.1
where the time goes:
time: 425 us; the launch traced here: 424 us
  blocking collectives  336 us (79%)
  waiting for transfers between devices  44.4 us (10%)
  between operations  13.5 us (3%)
  local copies, waits for them, and re-layouts  12.3 us (3%)
  matrix products  12.1 us (3%)
  loops' own time  5.51 us (1%)
    psum x8, blocking collectives, advance(): total = lax.psum(partial_value, ('col', 'row'))  336 us
    all_gather x1, waiting for transfers between devices, per_device(): lax.all_gather(child_solution, 'row', axis=0, tiled=True)  43.7 us
    dynamic_slice x8, local copies, waits for them, and re-layouts, advance(): flag = lax.dynamic_index_in_dim(flags, my_block, 0, keepdims=False)  10.5 us
  transfers between devices with their start and end apart: 1, of which 1 were waited for; matrix products, arithmetic and copies ran while one was open for 0% of the time, Pallas kernels for 0%

commit v1 on v0

--- a/solution.py
+++ b/solution.py
@@ -44,7 +44,7 @@
         partial_value = partial_value + lax.dynamic_index_in_dim(update, j_arow, 0, keepdims=False)
         partial_value = jnp.where(my_block == j, placed, jnp.zeros_like(placed)) - partial_value
         partial_value = jnp.where(row_index == j_row, partial_value, jnp.zeros_like(partial_value))
-        total = lax.psum(partial_value, ("col", "row"))
+        total = lax.psum(lax.psum(partial_value, "row"), "col")
         fresh = jnp.dot(
             inv_rows, total.astype(jnp.bfloat16), preferred_element_type=jnp.float32
         ).astype(jnp.bfloat16)

time: 425 us -> 653 us (1.54)
  waiting for transfers between devices: 44.4 us -> 277 us
  blocking collectives: 336 us -> 325 us
    psum x0 -> x8, waiting for transfers between devices: none -> 233 us  [advance(): total = lax.psum(lax.psum(partial_value, 'row'), 'col')]
    psum x8, blocking collectives: 336 us -> 325 us  [advance(): total = lax.psum(lax.psum(partial_value, 'row'), 'col')]
  transfers between devices with their start and end apart: 1 -> 9, of which waited for: 1 -> 9; matrix products, arithmetic and copies ran while one was open for 0% -> 0% of each run, Pallas kernels for 0% -> 0%
where the time goes in v1:
time: 653 us; the launch traced here: 652 us
  blocking collectives  325 us (50%)
  waiting for transfers between devices  277 us (42%)
  matrix products  17.7 us (3%)
  between operations  13.2 us (2%)
  local copies, waits for them, and re-layouts  12.3 us (2%)
    psum x8, blocking collectives, advance(): total = lax.psum(lax.psum(partial_value, 'row'), 'col')  325 us
    psum x8, waiting for transfers between devices, advance(): total = lax.psum(lax.psum(partial_value, 'row'), 'col')  233 us
    all_gather x1, waiting for transfers between devices, per_device(): lax.all_gather(child_solution, 'row', axis=0, tiled=True)  43.7 us
  transfers between devices with their start and end apart: 9, of which 9 were waited for; matrix products, arithmetic and copies ran while one was open for 0% of the time, Pallas kernels for 0%

profile of v1, /device:TPU:0, one launch (start us, length us, event | category | flops | bytes accessed | tf_op | source)
XLA Modules:
  0.0 651.6 jit_solution(13123749664838434350)
XLA Ops:
  6.5 0.7 all-gather.2.cloned.1.call-update
  7.3 1.1 copy.7
  8.4 43.7 %all-gather.2.cloned.1.call-done = bf16[10240,256]{1,0:T(8,128)(2,1)} async-done(((bf16[2560,256]{1,0:T(8,128)(2,1)}), bf16[10240,256]{1,0:T(8,128)(2,1)}) %all-gather.2.cloned.1.call-update) | async-done | bytes 5242896 | tf_op jit(solution)/shard_map/all_gather | solution.py:24
  52.1 8.4 %fusion.12 = f32[2,256,256]{1,2,0:T(8,128)S(1)} fusion(bf16[2,1,256,10240]{3,2,1,0:T(8,128)(2,1)} %param.9, bf16[10240,256]{1,0:T(8,128)(2,1)} %all-gather.2.cloned.1.call-done), kind=kOutput, calls=%fused_computation.15 | convolution fusion | flops 2684354560 | bytes 16252928 | tf_op jit(solution)/shard_map/dot_general | solution.py:22
  60.5 583.9 %while.17 = (s32[]{:T(128)}, bf16[256,256]{0,1:T(8,128)(2,1)S(1)}, s32[]{:T(128)}, s32[]{:T(128)}, f32[256,256]{0,1:T(8,128)S(1)}, /*index=5*/bf16[2,256,256]{2,...) while((s32[]{:T(128)}, bf16[256,256]{0,1:T(8,128)(2,1)S(1)}, ...), condition=%wide.region_3.4_spmd.clone, body=%wide.region_0.3_spmd.clone.sunk | while | flops 67829784 | bytes 3542448 | solution.py:54
  60.5 0.0 all-reduce.3.cloned.1.call-start
  60.6 1.3 dynamic_slice.47
  62.5 0.9 fusion.27
  63.5 32.2 %all-reduce.3.cloned.1.call-done = f32[256,256]{0,1:T(8,128)} async-done(((f32[256,256]{0,1:T(8,128)}), f32[256,256]{0,1:T(8,128)}) %all-reduce.3.cloned.1.call-update) | async-done | bytes 262160 | tf_op jit(solution)/shard_map/while/body/eval_jaxpr/psum | solution.py:47
  95.7 40.6 %all-reduce.4 = bf16[256,256]{0,1:T(8,128)(2,1)S(1)} all-reduce(f32[256,256]{0,1:T(8,128)} %all-reduce.3.cloned.1.call-done), channel_id=1, replica_groups=mesh['col'=8,'row'=4] {'col'}, use_global_device_ids=true, to_apply=%region_2.2 | all-reduce | flops 65536 | bytes 393216 | tf_op jit(solution)/shard_map/while/body/eval_jaxpr/psum | solution.py:47
  136.3 0.2 fusion.28
  136.7 1.3 dynamic_slice.47
  138.6 0.9 fusion.27
  139.6 28.7 %all-reduce.3.cloned.1.call-done = f32[256,256]{0,1:T(8,128)} async-done(((f32[256,256]{0,1:T(8,128)}), f32[256,256]{0,1:T(8,128)}) %all-reduce.3.cloned.1.call-update) | async-done | bytes 262160 | tf_op jit(solution)/shard_map/while/body/eval_jaxpr/psum | solution.py:47
  168.3 40.6 %all-reduce.4 = bf16[256,256]{0,1:T(8,128)(2,1)S(1)} all-reduce(f32[256,256]{0,1:T(8,128)} %all-reduce.3.cloned.1.call-done), channel_id=1, replica_groups=mesh['col'=8,'row'=4] {'col'}, use_global_device_ids=true, to_apply=%region_2.2 | all-reduce | flops 65536 | bytes 393216 | tf_op jit(solution)/shard_map/while/body/eval_jaxpr/psum | solution.py:47
  208.9 0.2 fusion.28
  209.2 0.0 all-reduce.3.cloned.1.call-start
  209.3 1.3 dynamic_slice.47
  211.2 0.9 fusion.27
  212.1 28.6 %all-reduce.3.cloned.1.call-done = f32[256,256]{0,1:T(8,128)} async-done(((f32[256,256]{0,1:T(8,128)}), f32[256,256]{0,1:T(8,128)}) %all-reduce.3.cloned.1.call-update) | async-done | bytes 262160 | tf_op jit(solution)/shard_map/while/body/eval_jaxpr/psum | solution.py:47
  240.7 40.6 %all-reduce.4 = bf16[256,256]{0,1:T(8,128)(2,1)S(1)} all-reduce(f32[256,256]{0,1:T(8,128)} %all-reduce.3.cloned.1.call-done), channel_id=1, replica_groups=mesh['col'=8,'row'=4] {'col'}, use_global_device_ids=true, to_apply=%region_2.2 | all-reduce | flops 65536 | bytes 393216 | tf_op jit(solution)/shard_map/while/body/eval_jaxpr/psum | solution.py:47
  281.4 0.2 fusion.28
  281.7 1.3 dynamic_slice.47
  283.7 0.9 fusion.27
  284.6 28.6 %all-reduce.3.cloned.1.call-done = f32[256,256]{0,1:T(8,128)} async-done(((f32[256,256]{0,1:T(8,128)}), f32[256,256]{0,1:T(8,128)}) %all-reduce.3.cloned.1.call-update) | async-done | bytes 262160 | tf_op jit(solution)/shard_map/while/body/eval_jaxpr/psum | solution.py:47
  313.2 40.6 %all-reduce.4 = bf16[256,256]{0,1:T(8,128)(2,1)S(1)} all-reduce(f32[256,256]{0,1:T(8,128)} %all-reduce.3.cloned.1.call-done), channel_id=1, replica_groups=mesh['col'=8,'row'=4] {'col'}, use_global_device_ids=true, to_apply=%region_2.2 | all-reduce | flops 65536 | bytes 393216 | tf_op jit(solution)/shard_map/while/body/eval_jaxpr/psum | solution.py:47
  353.9 0.2 fusion.28
  354.2 1.3 dynamic_slice.47
  356.2 0.9 fusion.27
  357.1 28.6 %all-reduce.3.cloned.1.call-done = f32[256,256]{0,1:T(8,128)} async-done(((f32[256,256]{0,1:T(8,128)}), f32[256,256]{0,1:T(8,128)}) %all-reduce.3.cloned.1.call-update) | async-done | bytes 262160 | tf_op jit(solution)/shard_map/while/body/eval_jaxpr/psum | solution.py:47
  385.7 40.6 %all-reduce.4 = bf16[256,256]{0,1:T(8,128)(2,1)S(1)} all-reduce(f32[256,256]{0,1:T(8,128)} %all-reduce.3.cloned.1.call-done), channel_id=1, replica_groups=mesh['col'=8,'row'=4] {'col'}, use_global_device_ids=true, to_apply=%region_2.2 | all-reduce | flops 65536 | bytes 393216 | tf_op jit(solution)/shard_map/while/body/eval_jaxpr/psum | solution.py:47
  426.4 0.2 fusion.28
  426.7 1.3 dynamic_slice.47
  428.7 0.9 fusion.27
  429.6 28.7 %all-reduce.3.cloned.1.call-done = f32[256,256]{0,1:T(8,128)} async-done(((f32[256,256]{0,1:T(8,128)}), f32[256,256]{0,1:T(8,128)}) %all-reduce.3.cloned.1.call-update) | async-done | bytes 262160 | tf_op jit(solution)/shard_map/while/body/eval_jaxpr/psum | solution.py:47
  458.3 40.6 %all-reduce.4 = bf16[256,256]{0,1:T(8,128)(2,1)S(1)} all-reduce(f32[256,256]{0,1:T(8,128)} %all-reduce.3.cloned.1.call-done), channel_id=1, replica_groups=mesh['col'=8,'row'=4] {'col'}, use_global_device_ids=true, to_apply=%region_2.2 | all-reduce | flops 65536 | bytes 393216 | tf_op jit(solution)/shard_map/while/body/eval_jaxpr/psum | solution.py:47
  499.0 0.2 fusion.28
  499.3 1.3 dynamic_slice.47
  501.2 0.9 fusion.27
  502.2 28.7 %all-reduce.3.cloned.1.call-done = f32[256,256]{0,1:T(8,128)} async-done(((f32[256,256]{0,1:T(8,128)}), f32[256,256]{0,1:T(8,128)}) %all-reduce.3.cloned.1.call-update) | async-done | bytes 262160 | tf_op jit(solution)/shard_map/while/body/eval_jaxpr/psum | solution.py:47
  530.9 40.6 %all-reduce.4 = bf16[256,256]{0,1:T(8,128)(2,1)S(1)} all-reduce(f32[256,256]{0,1:T(8,128)} %all-reduce.3.cloned.1.call-done), channel_id=1, replica_groups=mesh['col'=8,'row'=4] {'col'}, use_global_device_ids=true, to_apply=%region_2.2 | all-reduce | flops 65536 | bytes 393216 | tf_op jit(solution)/shard_map/while/body/eval_jaxpr/psum | solution.py:47
  571.5 0.2 fusion.28
  571.9 1.3 dynamic_slice.47
  573.8 0.9 fusion.27
  574.8 28.7 %all-reduce.3.cloned.1.call-done = f32[256,256]{0,1:T(8,128)} async-done(((f32[256,256]{0,1:T(8,128)}), f32[256,256]{0,1:T(8,128)}) %all-reduce.3.cloned.1.call-update) | async-done | bytes 262160 | tf_op jit(solution)/shard_map/while/body/eval_jaxpr/psum | solution.py:47
  603.4 40.6 %all-reduce.4 = bf16[256,256]{0,1:T(8,128)(2,1)S(1)} all-reduce(f32[256,256]{0,1:T(8,128)} %all-reduce.3.cloned.1.call-done), channel_id=1, replica_groups=mesh['col'=8,'row'=4] {'col'}, use_global_device_ids=true, to_apply=%region_2.2 | all-reduce | flops 65536 | bytes 393216 | tf_op jit(solution)/shard_map/while/body/eval_jaxpr/psum | solution.py:47
  644.1 0.2 fusion.28
  644.4 0.8 copy.9
  (20 shorter events, 0.4 us)
Async XLA Ops:
  6.5 45.5 %all-gather.2.cloned.1.call-start = ((), (), s32[]{:S(2)}) async-start(), calls=%async_computation | async-start | bytes 6553600 | tf_op jit(solution)/shard_map/all_gather | solution.py:24
  8.4 52.1 %copy-start = (bf16[2,1,256,1,256]{4,2,3,1,0:T(8,128)(2,1)S(1)}, bf16[2,1,256,1,256]{4,2,3,1,0:T(8,128)(2,1)}, u32[]{:S(2)}) copy-start(bf16[2,1,256,1,256]{4,2,3,1,0:T(8,128)(2,1)} %param.11) | copy-start | bytes 786436
  8.4 52.1 %copy-start.1 = (bf16[1,256,256]{2,1,0:T(8,128)(2,1)S(1)}, bf16[1,256,256]{2,1,0:T(8,128)(2,1)}, u32[]{:S(2)}) copy-start(bf16[1,256,256]{2,1,0:T(8,128)(2,1)} %param.13) | copy-start | bytes 393220
  60.5 35.2 %all-reduce.3.cloned.1.call-start = ((), (), s32[]{:S(2)}) async-start(), calls=%async_computation.1 | async-start | bytes 524288 | tf_op jit(solution)/shard_map/while/body/eval_jaxpr/psum | solution.py:47
  136.6 31.7 %all-reduce.3.cloned.1.call-start = ((), (), s32[]{:S(2)}) async-start(), calls=%async_computation.1 | async-start | bytes 524288 | tf_op jit(solution)/shard_map/while/body/eval_jaxpr/psum | solution.py:47
  209.2 31.6 %all-reduce.3.cloned.1.call-start = ((), (), s32[]{:S(2)}) async-start(), calls=%async_computation.1 | async-start | bytes 524288 | tf_op jit(solution)/shard_map/while/body/eval_jaxpr/psum | solution.py:47
  281.7 31.6 %all-reduce.3.cloned.1.call-start = ((), (), s32[]{:S(2)}) async-start(), calls=%async_computation.1 | async-start | bytes 524288 | tf_op jit(solution)/shard_map/while/body/eval_jaxpr/psum | solution.py:47
  354.1 31.6 %all-reduce.3.cloned.1.call-start = ((), (), s32[]{:S(2)}) async-start(), calls=%async_computation.1 | async-start | bytes 524288 | tf_op jit(solution)/shard_map/while/body/eval_jaxpr/psum | solution.py:47
  426.6 31.7 %all-reduce.3.cloned.1.call-start = ((), (), s32[]{:S(2)}) async-start(), calls=%async_computation.1 | async-start | bytes 524288 | tf_op jit(solution)/shard_map/while/body/eval_jaxpr/psum | solution.py:47
  499.2 31.7 %all-reduce.3.cloned.1.call-start = ((), (), s32[]{:S(2)}) async-start(), calls=%async_computation.1 | async-start | bytes 524288 | tf_op jit(solution)/shard_map/while/body/eval_jaxpr/psum | solution.py:47
  571.8 31.7 %all-reduce.3.cloned.1.call-start = ((), (), s32[]{:S(2)}) async-start(), calls=%async_computation.1 | async-start | bytes 524288 | tf_op jit(solution)/shard_map/while/body/eval_jaxpr/psum | solution.py:47
Sparse Core Ops, SparseCore 0:
  8.9 43.1 all-gather.1
  63.7 31.9 all-reduce.2
  139.8 28.4 all-reduce.2
  212.3 28.4 all-reduce.2
  284.7 28.4 all-reduce.2
  357.2 28.4 all-reduce.2
  429.8 28.4 all-reduce.2
  502.4 28.4 all-reduce.2
  575.0 28.4 all-reduce.2
